TPU v7x, 32 devices: a whole 2x2x4 slice. The times are simulated.
32 devices in a mesh: groups: 2 (over y), tok: 4 (over z), cache: 2 (over x), rep: 2 (over core).
Axes of the slice: x: 2, y: 2, z: 4, core: 2. Of those that a mesh axis runs over, the one named last changes fastest.
Arguments:
- x_in: bfloat16 [16, 512, 8192], P(('groups', 'rep'), 'tok', 'cache'), parts along dimension 0, may hold values from -6 to 6
- z_in: bfloat16 [16, 512, 8192], P(('groups', 'rep'), 'tok', 'cache'), parts along dimension 0, may hold values from -6 to 6
- b_in: bfloat16 [16, 512, 8, 128], P(('groups', 'rep'), 'tok', 'cache'), parts along dimension 0, may hold values from -6 to 6
- c_in: bfloat16 [16, 512, 8, 128], P(('groups', 'rep'), 'tok', 'cache'), parts along dimension 0, may hold values from -6 to 6
- dt_in: bfloat16 [16, 512, 128], P(('groups', 'rep'), 'tok', 'cache'), parts along dimension 0, may hold values from -2 to 10
- dt_bias: float32 [128], P('cache'), may hold values from -14 to -2
- a_log: float32 [128], P('cache'), may hold values from 0 to 3
- skip_gain: float32 [128], P('cache'), may hold values from 0.5 to 1.5
- norm_w: float32 [8192], P('cache'), may hold values from 0.5 to 1.5
- cache_states: float32 [8, 2, 64, 64, 128], P(('groups', 'cache'), None, 'tok'), parts along dimension 0, may hold values from -0.3 to 0.3
- parent: int32 [16], P('groups'), parts along dimension 0, may hold values from 0 to 3
- state_dev: int32 [8], P('groups'), parts along dimension 0, may hold values from 0 to 1, as said below
- state_slot: int32 [8], P('groups'), parts along dimension 0, may hold values from 0 to 1
- spans: int32 [16], P('groups'), parts along dimension 0, may hold values from 1 to 4
Outputs:
- y_out: bfloat16 [16, 512, 8192], P(('groups', 'rep'), 'tok', 'cache'), parts along dimension 0
- final_states: float32 [16, 128, 64, 128], P(('groups', 'rep'), ('cache', 'tok')), parts along dimension 0
There are 2 independent parts, one for each index of `groups`. A program takes and returns all parts, laid end to end along the dimension named above; an argument that names none is the same for every part. Nothing has to cross between parts.
Inputs may be any that keep to these rules, and one draw needn't show every extreme that they name: state_dev and state_slot together name every pair of a cache index and a slot exactly once.
All inputs are finite; a program needn't handle non-finite values.
Results may differ from a plain program's by a relative error of at most 0.0075.
Values may be sent and summed in bfloat16 or wider, within the bound.
A program may use at most 128 MiB of HBM per device.

v0:
```python
import jax
import jax.numpy as jnp
from jax import lax
from jax.sharding import PartitionSpec as P

HEADS = 128
HEAD_DIM = 64
GROUPS = 8
SPAN = 128


EPS = 1e-05


def span_scan(x_heads, step_size, b_group, c_group, decay_scale, skip_here, initial):
    requests, length, heads_here = step_size.shape
    blocks = length // SPAN
    head_channel_width = x_heads.shape[2] // heads_here
    x_blocks = x_heads.reshape(requests, blocks, SPAN, heads_here, head_channel_width)
    step_blocks = step_size.reshape(requests, blocks, SPAN, heads_here).transpose(0, 1, 3, 2)
    cum_rate = jnp.cumsum(-decay_scale[:, None] * step_blocks, axis=3)
    b_blocks = b_group.reshape(requests, blocks, SPAN, -1)
    c_blocks = c_group.reshape(requests, blocks, SPAN, -1)
    scores = jnp.einsum("mkin,mkjn->mkij", c_blocks, b_blocks, preferred_element_type=jnp.float32)
    causal = jnp.arange(SPAN)[:, None] >= jnp.arange(SPAN)[None, :]
    spread = cum_rate[..., :, None] - cum_rate[..., None, :]
    decay_mask = jnp.where(causal, jnp.exp(jnp.where(causal, spread, 0.0)), 0.0)
    blend_factors = (scores[:, :, None] * decay_mask * step_blocks[..., None, :]).astype(
        jnp.bfloat16
    )
    diagonal = jnp.einsum(
        "mkhij,mkjhp->mkihp", blend_factors, x_blocks, preferred_element_type=jnp.float32
    )
    weight = jnp.exp(cum_rate[..., -1:] - cum_rate) * step_blocks
    scaled = (b_blocks.astype(jnp.float32)[:, :, None] * weight[..., None]).astype(jnp.bfloat16)
    block_states = jnp.einsum(
        "mkjhp,mkhjn->mkhpn", x_blocks, scaled, preferred_element_type=jnp.float32
    )
    running_totals = cum_rate[..., -1]

    def advance(carried, step_inputs):
        block_total, new_state = step_inputs
        return (jnp.exp(block_total)[..., None, None] * carried + new_state, carried)

    final_state, before = lax.scan(
        advance, initial, (jnp.moveaxis(running_totals, 1, 0), jnp.moveaxis(block_states, 1, 0))
    )
    c_float = c_blocks.astype(jnp.float32)
    carried_in = jnp.einsum("mkin,kmhpn->mkihp", c_float, before, precision=lax.Precision.HIGHEST)
    growth = jnp.exp(cum_rate).transpose(0, 1, 3, 2)[..., None]
    combined = diagonal + carried_in * growth + skip_here[:, None] * x_blocks.astype(jnp.float32)
    return (combined, final_state, c_float, cum_rate, running_totals)


def fetch_parents(cache_states, own_slot, owner_dev):
    owned = owner_dev == lax.axis_index("cache")
    owned_terms = jnp.where(owned[:, None, None, None, None], cache_states[own_slot], 0.0)
    parent_share = lax.psum_scatter(
        owned_terms.astype(jnp.bfloat16), "cache", scatter_dimension=1, tiled=True
    ).astype(jnp.float32)
    return parent_share[:, 0]


def shards(
    x_in,
    z_in,
    b_in,
    c_in,
    dt_in,
    dt_bias,
    a_log,
    skip_gain,
    norm_w,
    cache_states,
    parent,
    state_dev,
    state_slot,
    spans,
):
    token_order = lax.axis_index("tok")
    replica_order = lax.axis_index("rep")
    tok_count = lax.axis_size("tok")
    requests, segment, channel_count = x_in.shape
    heads_here = dt_in.shape[2] // tok_count
    length = segment * tok_count
    x_heads, step_raw = (
        lax.all_to_all(x_in, "tok", split_axis=2, concat_axis=1, tiled=True),
        lax.all_to_all(dt_in, "tok", split_axis=2, concat_axis=1, tiled=True),
    )
    b_full, c_full = (
        lax.all_gather(b_in, "tok", axis=1, tiled=True),
        lax.all_gather(c_in, "tok", axis=1, tiled=True),
    )
    group_pick = token_order * heads_here // (HEADS // GROUPS)
    b_group = lax.dynamic_index_in_dim(b_full, group_pick, axis=2, keepdims=False)
    c_group = lax.dynamic_index_in_dim(c_full, group_pick, axis=2, keepdims=False)
    first_head = token_order * heads_here
    bias_here = lax.dynamic_slice_in_dim(dt_bias, first_head, heads_here)
    decay_scale = jnp.exp(lax.dynamic_slice_in_dim(a_log, first_head, heads_here))
    skip_here = lax.dynamic_slice_in_dim(skip_gain, first_head, heads_here)
    parent_here = lax.dynamic_slice_in_dim(parent, replica_order * requests, requests)
    span_here = lax.dynamic_slice_in_dim(spans, replica_order * requests, requests)
    valid_mask = (jnp.arange(length)[None, :] < span_here[:, None] * SPAN).astype(jnp.float32)
    step_size = jax.nn.softplus(step_raw.astype(jnp.float32) + bias_here) * valid_mask[..., None]
    slot_count = cache_states.shape[0]
    id_match = parent_here[:, None] == jnp.arange(state_dev.shape[0])[None, :]
    holder_row = jnp.sum(
        jnp.where(id_match, state_dev[None, :] * slot_count + state_slot[None, :], 0), axis=1
    )
    owner_dev = holder_row // slot_count
    own_slot = holder_row % slot_count
    initial = fetch_parents(cache_states, own_slot, owner_dev)
    combined, final_state, c_float, cum_rate, running_totals = span_scan(
        x_heads, step_size, b_group, c_group, decay_scale, skip_here, initial
    )
    ssd = combined.astype(jnp.bfloat16).reshape(requests, length, -1)
    returned = lax.all_to_all(ssd, "tok", split_axis=1, concat_axis=2, tiled=True)
    gated = returned.astype(jnp.float32) * jax.nn.silu(z_in.astype(jnp.float32))
    group_width = HEADS * HEAD_DIM // GROUPS
    grouped = gated.reshape(requests, segment, channel_count // group_width, group_width)
    inverse_rms = lax.rsqrt(jnp.mean(grouped * grouped, axis=-1, keepdims=True) + EPS)
    valid_here = lax.dynamic_slice_in_dim(valid_mask, token_order * segment, segment, 1)
    result = (
        (grouped * inverse_rms).reshape(requests, segment, channel_count)
        * norm_w
        * valid_here[..., None]
    )
    return (result.astype(jnp.bfloat16), final_state)


def solution(mesh):
    placed = (
        P(("groups", "rep"), "tok", "cache"),
        P(("groups", "rep"), "tok", "cache"),
        P(("groups", "rep"), "tok", "cache", None),
        P(("groups", "rep"), "tok", "cache", None),
        P(("groups", "rep"), "tok", "cache"),
        P("cache"),
        P("cache"),
        P("cache"),
        P("cache"),
        P(("groups", "cache"), None, "tok", None, None),
        P("groups"),
        P("groups"),
        P("groups"),
        P("groups"),
    )
    return jax.shard_map(
        shards,
        mesh=mesh,
        in_specs=placed,
        out_specs=(
            P(("groups", "rep"), "tok", "cache"),
            P(("groups", "rep"), ("cache", "tok"), None, None),
        ),
        check_vma=False,
    )
```

profile of v0, /device:TPU:24, one launch (start us, length us, event | category | flops | bytes accessed | tf_op | source)
XLA Modules:
  0.0 397.6 jit_solution(4447523708625058947)
XLA Ops:
  12.0 3.7 select_convert_fusion
  17.4 5.1 %all-to-all-start = ((bf16[4,128,64]{1,0,2:T(4,128)(2,1)}), bf16[4,128,64]{1,0,2:T(4,128)(2,1)S(1)}, u32[]{:S(2)}, u32[]{:S(2)}) async-start(bf16[4,128,64]{1,0,2:T(4,128)(2,1)} %copy.71), calls=%async_computation | async-start | bytes 131072 | tf_op jit(solution)/shard_map/all_to_all | solution.py:88
  22.5 7.7 %copy.73 = bf16[4,128,4096]{1,0,2:T(4,128)(2,1)} copy(bf16[4,128,4096]{2,1,0:T(8,128)(2,1)} %param.16) | data formatting | bytes 8388608 | tf_op args[0]
  30.2 5.1 %all-to-all-start.1 = ((bf16[4,128,4096]{1,0,2:T(4,128)(2,1)}), bf16[4,128,4096]{1,0,2:T(4,128)(2,1)}, u32[]{:S(2)}, u32[]{:S(2)}) async-start(bf16[4,128,4096]{1,0,2:T(4,128)(2,1)} %copy.73), calls=%async_computation.1 | async-start | bytes 8388608 | tf_op jit(solution)/shard_map/all_to_all | solution.py:87
  38.0 4.6 %reduce_window_sum.11 = f32[4,4,16,128]{3,2,1,0:T(8,128)S(1)} reduce-window(f32[4,4,16,128]{3,2,1,0:T(8,128)S(1)} %broadcast_multiply_fusion, f32[]{:T(128)} %constant.90.clone.1), window={size=1x1x1x128 pad=0_0x0_0x0_0x127_0}, to_apply=%region_0.1 | reduce-window | flops 4161536 | bytes 262148 | tf_op jit(solution)/shard_map/jit(cumsum)/reduce_window_sum | solution.py:21
  43.6 36.2 %all-reduce.3.cloned.1.call-done = bf16[4,2,16,64,128]{4,3,2,1,0:T(8,128)(2,1)} async-done(((bf16[4,2,16,64,128]{4,3,2,1,0:T(8,128)(2,1)}), bf16[4,2,16,64,128]{4,3,2,1,0:T(8,128)(2,1)}) %all-reduce.3.cloned.1.call-update) | async-done | bytes 2097168
  81.8 4.8 %all-gather.5.cloned.1.call-done = bf16[4,512,4,128]{3,1,0,2:T(8,128)(2,1)} async-done(((bf16[4,128,4,128]{3,1,0,2:T(8,128)(2,1)}), bf16[4,512,4,128]{3,1,0,2:T(8,128)(2,1)}) %all-gather.5.cloned.1.call-update) | async-done | bytes 2097168 | tf_op jit(solution)/shard_map/all_gather | solution.py:91
  88.8 91.3 %all-gather.3.cloned.1.call-done = bf16[4,512,4,128]{3,1,0,2:T(8,128)(2,1)} async-done(((bf16[4,128,4,128]{3,1,0,2:T(8,128)(2,1)}), bf16[4,512,4,128]{3,1,0,2:T(8,128)(2,1)}) %all-gather.3.cloned.1.call-update) | async-done | bytes 2097168 | tf_op jit(solution)/shard_map/all_gather | solution.py:92
  185.4 3.1 copy.74
  190.5 8.1 %fusion.19 = f32[4,4,16,64,128]{4,3,2,0,1:T(8,128)} fusion(bf16[4,4,128,16,64]{2,4,3,1,0:T(8,128)(2,1)S(1)} %bitcast.111, f32[4,4,16,128]{3,2,1,0:T(8,128)S(1)} %get-tuple-element.81, f32[4,4,128,128]{3,2,1,0:T(8,128)S(1)} %copy-done.7), kind=kOutput, calls=%fused_computation.33 | convolution fusion | flops 545259520 | bytes 13762560 | tf_op jit(solution)/shard_map/mkjhp,mkhjn->mkhpn/dot_general | solution.py:36
  198.6 14.2 %while.12 = (s32[]{:T(128)}, f32[4,16,64,128]{3,2,1,0:T(8,128)S(1)}, f32[4,4,16,64,128]{4,3,2,0,1:T(8,128)}, f32[4,4,16]{2,0,1:T(4,128)S(1)}, f32[4,4,16,64,128]{4,3,2,0,1:T(8,128)}, /*index=5*/s32[]{:T(128)}) while((s32[]{:T(128)}, f32[4,16,64,128]{3,2,1,0:T(8,128)S(1)}, f32[4,4,16,64,128]{4,3,2,0,1:T(8,128)}, f32[4,4,16]{2,0,1:T(4,128)S(1)}, ...), condition=%wide.region_4.5_spmd, body=%wide.region_3.4_spmd.sunk | while | flops 1048578 | bytes 10487629 | solution.py:45
  212.9 7.2 %fusion.34 = f32[4,4,128,16,64]{2,4,3,1,0:T(8,128)S(1)} fusion(bf16[4,4,128,128,1]{3,2,4,1,0:T(8,128)(2,1)S(1)} %bitcast.114, f32[4,4,16,64,128]{4,3,2,0,1:T(8,128)} %get-tuple-element.30), kind=kOutput, calls=%fused_computation.76 | convolution fusion | flops 3221225472 | bytes 17301504 | tf_op jit(solution)/shard_map/mkin,kmhpn->mkihp/dot_general | solution.py:49
  220.2 9.1 %fusion.10 = bf16[4,4,128,16,64]{2,4,3,1,0:T(8,128)(2,1)} fusion(bf16[4,4,128,16,64]{2,4,3,1,0:T(8,128)(2,1)S(1)} %bitcast.112, f32[4,4,128,16,64]{2,4,3,1,0:T(8,128)S(1)} %fusion.34, f32[16]{0:T(128)S(1)} %dynamic_slice.39, f32[4,4,128,16]{2,3,1,0:T(8,128)S(1)} %get-tuple-element.80, f32[4,4,16,128]{3,2,1,0:T(8,128)S(1)} %copy-done.11, ...), kind=kOutput, calls=%fused_computation.23 | convolution fusion | flops 574619648 | bytes 18235456 | tf_op jit(solution)/shard_map/mkhij,mkjhp->mkihp/dot_general | solution.py:31
  229.4 13.0 %copy.85 = bf16[4,4,128,16,64]{4,3,0,2,1:T(8,128)(2,1)} copy(bf16[4,4,128,16,64]{2,4,3,1,0:T(8,128)(2,1)} %fusion.10) | data formatting | bytes 8388608 | tf_op jit(solution)/shard_map/reshape | solution.py:116
  242.4 12.8 %reshape.172 = bf16[4,512,1024]{2,0,1:T(4,128)(2,1)} reshape(bf16[4,4,128,16,64]{4,3,0,2,1:T(8,128)(2,1)} %copy.85) | data formatting | bytes 8388608 | tf_op jit(solution)/shard_map/reshape | solution.py:116
  255.1 7.7 %all-to-all-start.2 = ((bf16[4,512,1024]{2,0,1:T(4,128)(2,1)}), bf16[4,512,1024]{2,0,1:T(4,128)(2,1)}, u32[]{:S(2)}, u32[]{:S(2)}) async-start(bf16[4,512,1024]{2,0,1:T(4,128)(2,1)} %reshape.172), calls=%async_computation.2 | async-start | bytes 8388608 | tf_op jit(solution)/shard_map/all_to_all | solution.py:117
  262.8 6.3 %copy.82 = bf16[4,128,4096]{1,2,0:T(8,128)(2,1)} copy(bf16[4,128,4096]{2,1,0:T(8,128)(2,1)} %param.17) | data formatting | bytes 8388608 | tf_op args[1]
  269.2 84.7 %all-to-all-done.2 = bf16[4,512,1024]{2,0,1:T(4,128)(2,1)} async-done(((bf16[4,512,1024]{2,0,1:T(4,128)(2,1)}), bf16[4,512,1024]{2,0,1:T(4,128)(2,1)}, u32[]{:S(2)}, u32[]{:S(2)}) %all-to-all-start.2) | async-done | bytes 4194336 | tf_op jit(solution)/shard_map/all_to_all | solution.py:117
  353.9 3.6 copy.80
  357.4 4.3 %convert_bitcast_fusion = f32[4,128,4,1024]{3,1,2,0:T(8,128)} fusion(bf16[4,4,128,1024]{3,2,1,0:T(8,128)(2,1)S(1)} %bitcast.110), kind=kLoop, calls=%fused_computation.15 | loop fusion | flops 2097152 | bytes 12582912 | tf_op jit(solution)/shard_map/convert_element_type | solution.py:118
  361.8 8.7 %copy.81 = f32[4,128,4,1024]{1,3,2,0:T(8,128)} copy(f32[4,128,4,1024]{3,1,2,0:T(8,128)} %convert_bitcast_fusion) | data formatting | bytes 16777216 | tf_op jit(solution)/shard_map/convert_element_type | solution.py:118
  370.5 7.2 %bitcast_reduce_fusion = f32[4,128,4]{1,2,0:T(4,128)S(1)} fusion(bf16[4,128,4096]{1,2,0:T(8,128)(2,1)} %copy.82, f32[4,128,4,1024]{1,3,2,0:T(8,128)} %copy.81), kind=kLoop, calls=%fused_computation.20 | loop fusion | flops 16775168 | bytes 12591104 | tf_op jit(solution)/shard_map/reduce_sum | solution.py:121
  378.7 5.1 %fusion.8 = bf16[4,128,4096]{1,2,0:T(8,128)(2,1)} fusion(f32[4,128]{1,0:T(4,128)S(1)} %fusion.28, f32[4096]{0:T(1024)S(1)} %copy-done.13, f32[4,128,4]{1,2,0:T(4,128)S(1)} %add_rsqrt_fusion, bf16[4,128,4096]{1,2,0:T(8,128)(2,1)S(1)} %copy-done.4, f32[4,128,4,1024]{1,3,2,0:T(8,128)S(1)} %copy-done.3), kind=kLoop, calls=%fused_computation.19 | loop fusion | flops 20971520 | bytes 16803840 | tf_op jit(solution)/shard_map/convert_element_type | solution.py:128
  383.8 6.3 %copy.83 = bf16[4,128,4096]{2,1,0:T(8,128)(2,1)} copy(bf16[4,128,4096]{1,2,0:T(8,128)(2,1)} %fusion.8) | data formatting | bytes 8388608
  (94 shorter events, 36.1 us)
Async XLA Ops:
  8.0 7.8 %copy-start.9 = (bf16[4,128,4,128]{3,2,1,0:T(4,128)(2,1)S(1)}, bf16[4,128,4,128]{3,2,1,0:T(4,128)(2,1)}, u32[]{:S(2)}) copy-start(bf16[4,128,4,128]{3,2,1,0:T(4,128)(2,1)} %param.18) | copy-start | bytes 1572868
  8.0 8.7 %copy-start.12 = (bf16[4,128,64]{1,2,0:T(8,128)(2,1)S(1)}, bf16[4,128,64]{1,2,0:T(8,128)(2,1)}, u32[]{:S(2)}) copy-start(bf16[4,128,64]{1,2,0:T(8,128)(2,1)} %param.20) | copy-start | bytes 196612
  8.0 71.8 %all-reduce.3.cloned.1.call-start = ((), (), s32[]{:S(2)}) async-start(), calls=%async_computation.5 | async-start | bytes 4194304
  15.7 70.9 %all-gather.5.cloned.1.call-start = ((), (), s32[]{:S(2)}) async-start(), calls=%async_computation.4 | async-start | bytes 2621440 | tf_op jit(solution)/shard_map/all_gather | solution.py:91
  17.4 12.8 %all-to-all-start = ((bf16[4,128,64]{1,0,2:T(4,128)(2,1)}), bf16[4,128,64]{1,0,2:T(4,128)(2,1)S(1)}, u32[]{:S(2)}, u32[]{:S(2)}) async-start(bf16[4,128,64]{1,0,2:T(4,128)(2,1)} %copy.71), calls=%async_computation | async-start | bytes 131072 | tf_op jit(solution)/shard_map/all_to_all | solution.py:88
  22.5 12.8 %copy-start.10 = (bf16[4,128,4,128]{3,2,1,0:T(4,128)(2,1)S(1)}, bf16[4,128,4,128]{3,2,1,0:T(4,128)(2,1)}, u32[]{:S(2)}) copy-start(bf16[4,128,4,128]{3,2,1,0:T(4,128)(2,1)} %param.19) | copy-start | bytes 1572868
  22.5 13.7 %copy-start.15 = (f32[64]{0:T(128)S(1)}, f32[64]{0:T(128)}, u32[]{:S(2)}) copy-start(f32[64]{0:T(128)} %param.21) | copy-start | bytes 772
  22.5 13.8 %copy-start.16 = (f32[64]{0:T(128)S(1)}, f32[64]{0:T(128)}, u32[]{:S(2)}) copy-start(f32[64]{0:T(128)} %param.23) | copy-start | bytes 772
  22.5 13.9 %copy-start.19 = (u32[32]{0:T(128)S(1)}, u32[32]{0:T(128)}, u32[]{:S(2)}) copy-start(u32[32]{0:T(128)} %constant.102) | copy-start | bytes 388
  22.5 14.5 %copy-start.17 = (f32[64]{0:T(128)S(1)}, f32[64]{0:T(128)}, u32[]{:S(2)}) copy-start(f32[64]{0:T(128)} %param.22) | copy-start | bytes 772
  22.5 14.6 %copy-start.18 = (s32[8]{0:T(128)S(1)}, s32[8]{0:T(128)}, u32[]{:S(2)}) copy-start(s32[8]{0:T(128)} %param.29) | copy-start | bytes 100
  30.2 155.2 %all-to-all-start.1 = ((bf16[4,128,4096]{1,0,2:T(4,128)(2,1)}), bf16[4,128,4096]{1,0,2:T(4,128)(2,1)}, u32[]{:S(2)}, u32[]{:S(2)}) async-start(bf16[4,128,4096]{1,0,2:T(4,128)(2,1)} %copy.73), calls=%async_computation.1 | async-start | bytes 8388608 | tf_op jit(solution)/shard_map/all_to_all | solution.py:87
  35.3 144.8 %all-gather.3.cloned.1.call-start = ((), (), s32[]{:S(2)}) async-start(), calls=%async_computation.3 | async-start | bytes 2621440 | tf_op jit(solution)/shard_map/all_gather | solution.py:92
  185.4 5.1 %copy-start.7 = (f32[4,4,128,128]{3,2,1,0:T(8,128)S(1)}, f32[4,4,128,128]{3,2,1,0:T(8,128)}, u32[]{:S(2)}) copy-start(f32[4,4,128,128]{3,2,1,0:T(8,128)} %convert_element_type.65) | copy-start | bytes 3145732
  212.9 7.3 %copy-start.2 = (f32[4,16,64,128]{3,2,1,0:T(8,128)}, f32[4,16,64,128]{3,2,1,0:T(8,128)S(1)}, u32[]{:S(2)}) copy-start(f32[4,16,64,128]{3,2,1,0:T(8,128)S(1)} %get-tuple-element.69) | copy-start | bytes 6291460
  212.9 7.3 %copy-start.6 = (bf16[4,128,4,1024]{1,3,2,0:T(8,128)(2,1)S(1)}, bf16[4,128,4,1024]{1,3,2,0:T(8,128)(2,1)}, u32[]{:S(2)}) copy-start(bf16[4,128,4,1024]{1,3,2,0:T(8,128)(2,1)} %copy-done.5) | copy-start | bytes 12582916
  212.9 7.3 %copy-start.8 = (f32[4,4,128,128]{3,2,1,0:T(8,128)S(1)}, f32[4,4,128,128]{3,2,1,0:T(8,128)}, u32[]{:S(2)}) copy-start(f32[4,4,128,128]{3,2,1,0:T(8,128)} %fusion.33) | copy-start | bytes 3145732
  212.9 7.3 %copy-start.11 = (f32[4,4,16,128]{3,2,1,0:T(8,128)S(1)}, f32[4,4,16,128]{3,2,1,0:T(8,128)}, u32[]{:S(2)}) copy-start(f32[4,4,16,128]{3,2,1,0:T(8,128)} %get-tuple-element.82) | copy-start | bytes 393220
  212.9 7.3 %copy-start.14 = (pred[128,128]{1,0:T(8,128)(4,1)S(1)}, pred[128,128]{1,0:T(8,128)(4,1)}, u32[]{:S(2)}) copy-start(pred[128,128]{1,0:T(8,128)(4,1)} %iota_compare_fusion) | copy-start | bytes 49156
  255.1 98.7 %all-to-all-start.2 = ((bf16[4,512,1024]{2,0,1:T(4,128)(2,1)}), bf16[4,512,1024]{2,0,1:T(4,128)(2,1)}, u32[]{:S(2)}, u32[]{:S(2)}) async-start(bf16[4,512,1024]{2,0,1:T(4,128)(2,1)} %reshape.172), calls=%async_computation.2 | async-start | bytes 8388608 | tf_op jit(solution)/shard_map/all_to_all | solution.py:117
  370.5 7.2 %copy-start.3 = (f32[4,128,4,1024]{1,3,2,0:T(8,128)S(1)}, f32[4,128,4,1024]{1,3,2,0:T(8,128)}, u32[]{:S(2)}) copy-start(f32[4,128,4,1024]{1,3,2,0:T(8,128)} %copy.81) | copy-start | bytes 25165828
  370.5 8.2 %copy-start.4 = (bf16[4,128,4096]{1,2,0:T(8,128)(2,1)S(1)}, bf16[4,128,4096]{1,2,0:T(8,128)(2,1)}, u32[]{:S(2)}) copy-start(bf16[4,128,4096]{1,2,0:T(8,128)(2,1)} %copy.82) | copy-start | bytes 12582916
  370.5 8.2 %copy-start.13 = (f32[4096]{0:T(1024)S(1)}, f32[4096]{0:T(1024)}, u32[]{:S(2)}) copy-start(f32[4096]{0:T(1024)} %param.24) | copy-start | bytes 49156
  378.7 11.5 %copy-start.1 = (f32[2,2,16,64,128]{4,3,2,1,0:T(8,128)S(1)}, f32[2,2,16,64,128]{4,3,2,1,0:T(8,128)}, u32[]{:S(2)}) copy-start(f32[2,2,16,64,128]{4,3,2,1,0:T(8,128)} %param.25) | copy-start | bytes 6291460
  (2 other events, 3.9 us)
Sparse Core Ops, SparseCore 0:
  15.8 63.9 all-reduce.2
Sparse Core Ops, SparseCore 1:
  17.8 68.8 all-gather.4
  88.1 91.9 all-gather.2
where the time goes:
time: 403 us; the launch traced here: 398 us
  waiting for transfers between devices  220 us (55%)
  local copies, waits for them, and re-layouts  79.3 us (20%)
  other arithmetic  38.7 us (10%)
  matrix products  26 us (6%)
  starting transfers between devices  17.9 us (4%)
  between operations  15.8 us (4%)
    all_gather x1, waiting for transfers between devices, shards(): lax.all_gather(c_in, 'tok', axis=1, tiled=True)  91.3 us
    all_to_all x1, waiting for transfers between devices, shards(): lax.all_to_all(ssd, 'tok', split_axis=1, concat_axis=2, tiled=True)  84.7 us
    unnamed x4, waiting for transfers between devices  36.2 us
    unnamed x47, local copies, waits for them, and re-layouts  26.5 us
    reshape x2, local copies, waits for them, and re-layouts, shards(): ssd = combined.astype(jnp.bfloat16).reshape(requests, length, -1)  25.8 us
    dot_general x1, matrix products, span_scan(): jnp.einsum('mkhij,mkjhp->mkihp', blend_factors, x_blocks, preferred_eleme...  9.13 us
    convert_element_type x1, local copies, waits for them, and re-layouts, shards(): gated = returned.astype(jnp.float32) * jax.nn.silu(z_in.astype(jnp.float32))  8.71 us
    dot_general x1, matrix products, span_scan(): jnp.einsum('mkjhp,mkhjn->mkhpn', x_blocks, scaled, preferred_element_type...  8.13 us
  transfers between devices with their start and end apart: 6, of which 5 were waited for; matrix products, arithmetic and copies ran while one was open for 8% of the time, Pallas kernels for 0%

commit v1 on v0

v1 whole, which is shorter than its diff:
```python
import functools

import jax
import jax.numpy as jnp
from jax import lax
from jax.experimental import pallas as pl
from jax.experimental.pallas import tpu as pltpu
from jax.sharding import PartitionSpec as P

HEADS = 128
HEAD_DIM = 64
STATE = 128
GROUPS = 8
SPAN = 128
PER_GROUP = HEADS // GROUPS
WIDTH = PER_GROUP * HEAD_DIM
CHUNK = 256
EPS = 1e-05
MESH = pl.DeviceIdType.MESH
F32 = jnp.float32
BF16 = jnp.bfloat16


def contract(a, b, da, db, precision=None):
    return lax.dot_general(
        a, b, (((da,), (db,)), ((), ())), precision=precision, preferred_element_type=F32
    )


def scan_kernel(
    tok_n,
    cache_n,
    requests,
    groups,
    slots,
    parent,
    state_dev,
    state_slot,
    spans,
    step_t,
    rate_t,
    skip_w,
    norm_w,
    x_in,
    z_in,
    b_in,
    c_in,
    kept_in,
    y_out,
    final_out,
    kept_send,
    kept,
    initial,
    carry_in,
    carry_out,
    final_in,
    local_state,
    direct,
    columns,
    totals,
    expand,
    upper,
    gated,
    kx_send,
    kx_recv,
    init_send,
    init_recv,
    chain_send,
    chain_recv,
    fin_send,
    fin_recv,
):
    t = lax.axis_index("tok")
    c = lax.axis_index("cache")
    rep = lax.axis_index("rep")
    last = tok_n - 1
    units = requests * groups
    pieces = tok_n // groups
    rows = WIDTH // pieces

    barrier = pltpu.get_barrier_semaphore()
    for d in range(1, tok_n):
        pl.semaphore_signal(
            barrier, inc=1, device_id={"tok": lax.rem(t + d, tok_n)}, device_id_type=MESH
        )
    for d in range(1, cache_n):
        pl.semaphore_signal(
            barrier, inc=1, device_id={"cache": lax.rem(c + d, cache_n)}, device_id_type=MESH
        )

    for s in range(slots):
        for i in range(cache_n):
            kept_send[i * slots + s] = kept_in[s, i].astype(BF16)
        kept[c * slots + s] = kept_in[s, c].astype(BF16)

    pl.semaphore_wait(barrier, tok_n + cache_n - 2)

    def kept_copy(d):
        peer = lax.rem(c + d, cache_n)
        return pltpu.make_async_remote_copy(
            src_ref=kept_send.at[pl.ds(peer * slots, slots)],
            dst_ref=kept.at[pl.ds(c * slots, slots)],
            send_sem=kx_send.at[d - 1],
            recv_sem=kx_recv.at[d - 1],
            device_id={"cache": peer},
            device_id_type=MESH,
        )

    def init_copy(r, unit, piece, owner):
        return pltpu.make_async_remote_copy(
            src_ref=initial.at[r],
            dst_ref=carry_in.at[unit, pl.ds(pl.multiple_of(piece * rows, rows), rows)],
            send_sem=init_send.at[r],
            recv_sem=init_recv.at[r, owner],
            device_id={"tok": 0},
            device_id_type=MESH,
        )

    def chain_copy(unit):
        return pltpu.make_async_remote_copy(
            src_ref=carry_out.at[unit],
            dst_ref=carry_in.at[unit],
            send_sem=chain_send.at[unit],
            recv_sem=chain_recv.at[unit],
            device_id={"tok": lax.rem(t + 1, tok_n)},
            device_id_type=MESH,
        )

    def final_copy(r, unit, piece, owner):
        return pltpu.make_async_remote_copy(
            src_ref=carry_out.at[unit, pl.ds(pl.multiple_of(piece * rows, rows), rows)],
            dst_ref=final_in.at[r],
            send_sem=fin_send.at[r, owner],
            recv_sem=fin_recv.at[r],
            device_id={"tok": owner},
            device_id_type=MESH,
        )

    def place(u):
        others = groups - 1
        first = u < requests
        later = jnp.int32(0)
        for k in range(1, requests):
            later = later + jnp.where(u >= requests + k * others, 1, 0).astype(jnp.int32)
        r = jnp.where(first, u, later)
        g = jnp.where(first, 0, u + (1 - requests) - later * others)
        return r, g

    def unit_of(r, g):
        return jnp.where(g == 0, r, requests + r * (groups - 1) + g - 1)

    def valid_of(r):
        return jnp.where(t < spans[rep * requests + r], 1.0, 0.0).astype(F32)

    for d in range(1, cache_n):
        kept_copy(d).start()

    row_i = lax.broadcasted_iota(jnp.int32, (SPAN, SPAN), 0)
    col_i = lax.broadcasted_iota(jnp.int32, (SPAN, SPAN), 1)
    upper[...] = jnp.where(row_i <= col_i, 1.0, 0.0).astype(F32)
    e_row = lax.broadcasted_iota(jnp.int32, (SPAN, WIDTH), 0)
    e_col = lax.broadcasted_iota(jnp.int32, (SPAN, WIDTH), 1)
    same = (e_row & (PER_GROUP - 1)) == (e_col // HEAD_DIM)
    block = e_row // PER_GROUP
    expand[0] = jnp.where(same & ((block == 1) | (block == 2)), 1.0, 0.0).astype(BF16)
    expand[1] = jnp.where(same & ((block == 3) | (block == 4)), 1.0, 0.0).astype(BF16)

    def prepare(u):
        r, g = place(u)
        heads = pl.ds(pl.multiple_of(g * PER_GROUP, PER_GROUP), PER_GROUP)
        lanes = pl.ds(pl.multiple_of(g * STATE, STATE), STATE)
        step = step_t[r, heads, :] * valid_of(r)
        cum = contract(rate_t[heads, :] * step, upper[...], 1, 0, lax.Precision.HIGHEST)
        total = cum[:, SPAN - 1 :]
        weight = jnp.exp(total - cum) * step
        growth = jnp.exp(cum)
        weight_hi = weight.astype(BF16).astype(F32)
        growth_hi = growth.astype(BF16).astype(F32)
        stacked = jnp.concatenate(
            [
                cum,
                weight_hi,
                weight - weight_hi,
                growth_hi,
                growth - growth_hi,
                jnp.zeros((SPAN - 5 * PER_GROUP, SPAN), F32),
            ],
            axis=0,
        )
        turned = stacked.T
        split = turned.astype(BF16)
        columns[...] = split
        totals[...] = jnp.broadcast_to(jnp.exp(total), (PER_GROUP, STATE))
        b_block = b_in[r, :, lanes]
        c_block = c_in[r, :, lanes]
        for k in range(WIDTH // CHUNK):
            here = pl.ds(pl.multiple_of(g * WIDTH + k * CHUNK, CHUNK), CHUNK)
            wide = contract(split, expand[0, :, k * CHUNK : (k + 1) * CHUNK], 1, 0)
            scaled = (x_in[r, :, here].astype(F32) * wide).astype(BF16)
            local_state[k * CHUNK : (k + 1) * CHUNK, :] = contract(scaled, b_block, 0, 0)
        scores = contract(c_block, b_block, 1, 1)
        scores = jnp.where(row_i >= col_i, scores, 0.0)
        low = jnp.where(lax.broadcasted_iota(jnp.int32, (1, SPAN), 1) < HEAD_DIM, 1.0, 0.0)
        low_mask = low.astype(BF16)
        high_mask = (1.0 - low).astype(BF16)
        for k in range(PER_GROUP // 2):
            mixes = []
            for h in (2 * k, 2 * k + 1):
                spread = turned[:, h : h + 1] - cum[h : h + 1, :]
                mix = scores * jnp.exp(jnp.minimum(spread, 0.0)) * step[h : h + 1, :]
                mixes.append(mix.astype(BF16))
            here = pl.ds(pl.multiple_of(g * WIDTH + k * SPAN, SPAN), SPAN)
            x_pair = x_in[r, :, here]
            x_split = jnp.concatenate([x_pair * low_mask, x_pair * high_mask], axis=0)
            out = contract(jnp.concatenate(mixes, axis=1), x_split, 1, 0)
            direct[:, k * SPAN : (k + 1) * SPAN] = out + skip_w[:, here] * x_pair.astype(F32)

    def advance(u):
        r, g = place(u)
        if tok_n > 1:

            @pl.when(t > 0)
            def _():
                chain_copy(u).wait_recv()

            for q in range(pieces):
                owner = g * pieces + q

                @pl.when((t == 0) & (owner != 0))
                def _():
                    init_copy(r, u, q, owner).wait_recv()

        for h in range(PER_GROUP):
            part = slice(h * HEAD_DIM, (h + 1) * HEAD_DIM)
            carried = carry_in[u, part, :].astype(F32) * totals[h : h + 1, :]
            carry_out[u, part, :] = (carried + local_state[part, :]).astype(BF16)

        @pl.when(t < last)
        def _():
            chain_copy(u).start()

        for q in range(pieces):
            owner = g * pieces + q

            @pl.when((t == last) & (owner != last))
            def _():
                final_copy(r, u, q, owner).start()

            @pl.when((t == last) & (owner == last))
            def _():
                final_out[r] = carry_out[u, q * rows : (q + 1) * rows, :].astype(F32)

        lanes = pl.ds(pl.multiple_of(g * STATE, STATE), STATE)
        c_block = c_in[r, :, lanes]
        split = columns[...]
        power = jnp.zeros((SPAN, 1), F32)
        for k in range(WIDTH // CHUNK):
            part = slice(k * CHUNK, (k + 1) * CHUNK)
            here = pl.ds(pl.multiple_of(g * WIDTH + k * CHUNK, CHUNK), CHUNK)
            wide = contract(split, expand[1, :, part], 1, 0)
            carried = contract(c_block, carry_in[u, part, :], 1, 1)
            ssd = (direct[:, part] + carried * wide).astype(BF16).astype(F32)
            gate = z_in[r, :, here].astype(F32)
            value = ssd * (gate / (1.0 + jnp.exp(-gate)))
            gated[:, part] = value
            power = power + jnp.sum(value * value, axis=1, keepdims=True)
        inverse = lax.rsqrt(power * (1.0 / WIDTH) + EPS) * valid_of(r)
        for k in range(WIDTH // CHUNK):
            part = slice(k * CHUNK, (k + 1) * CHUNK)
            here = pl.ds(pl.multiple_of(g * WIDTH + k * CHUNK, CHUNK), CHUNK)
            y_out[r, :, here] = (gated[:, part] * inverse * norm_w[:, here]).astype(BF16)

    for d in range(1, cache_n):
        kept_copy(d).wait_recv()
    my_group = t // pieces
    my_piece = lax.rem(t, pieces)
    for r in range(requests):
        kept_id = parent[rep * requests + r]
        row = state_dev[kept_id] * slots + state_slot[kept_id]
        state = kept[row]

        @pl.when(t == 0)
        def _():
            carry_in[r, 0:rows, :] = state

        @pl.when(t > 0)
        def _():
            initial[r] = state
            init_copy(r, unit_of(r, my_group), my_piece, t).start()

    @pl.loop(0, units)
    def _(u):
        prepare(u)
        advance(u)

    @pl.when(t < last)
    def _():
        for r in range(requests):
            final_copy(r, unit_of(r, my_group), my_piece, t).wait_recv()
            final_out[r] = final_in[r].astype(F32)

        @pl.loop(0, units)
        def _(u):
            chain_copy(u).wait_send()

    @pl.when(t > 0)
    def _():
        for r in range(requests):
            init_copy(r, unit_of(r, my_group), my_piece, t).wait_send()

    @pl.when(t == last)
    def _():
        @pl.loop(0, units)
        def _(u):
            r, g = place(u)
            for q in range(pieces):
                owner = g * pieces + q

                @pl.when(owner != last)
                def _():
                    final_copy(r, u, q, owner).wait_send()

    for d in range(1, cache_n):
        kept_copy(d).wait_send()


def shards(
    x_in,
    z_in,
    b_in,
    c_in,
    dt_in,
    dt_bias,
    a_log,
    skip_gain,
    norm_w,
    cache_states,
    parent,
    state_dev,
    state_slot,
    spans,
):
    tok_n = lax.axis_size("tok")
    cache_n = lax.axis_size("cache")
    requests, segment, channels = x_in.shape
    groups = channels // WIDTH
    heads = groups * PER_GROUP
    slots = cache_states.shape[0]
    units = requests * groups
    owned = heads // tok_n * HEAD_DIM
    step_t = jax.nn.softplus(dt_in.astype(F32) + dt_bias).transpose(0, 2, 1)
    rate_t = jnp.broadcast_to(-jnp.exp(a_log)[:, None], (heads, SPAN))
    skip_w = jnp.repeat(skip_gain, HEAD_DIM)[None, :]
    vmem = pl.BlockSpec(memory_space=pltpu.VMEM)
    smem = pl.BlockSpec(memory_space=pltpu.SMEM)
    dma = pltpu.SemaphoreType.DMA
    y_out, final_states = pl.pallas_call(
        functools.partial(scan_kernel, tok_n, cache_n, requests, groups, slots),
        out_shape=(
            jax.ShapeDtypeStruct((requests, segment, channels), BF16),
            jax.ShapeDtypeStruct((requests, owned, STATE), F32),
        ),
        in_specs=[smem] * 4 + [vmem] * 9,
        out_specs=(vmem, vmem),
        scratch_shapes=[
            pltpu.VMEM((cache_n * slots, owned, STATE), BF16),
            pltpu.VMEM((cache_n * slots, owned, STATE), BF16),
            pltpu.VMEM((requests, owned, STATE), BF16),
            pltpu.VMEM((units, WIDTH, STATE), BF16),
            pltpu.VMEM((units, WIDTH, STATE), BF16),
            pltpu.VMEM((requests, owned, STATE), BF16),
            pltpu.VMEM((WIDTH, STATE), F32),
            pltpu.VMEM((SPAN, WIDTH), F32),
            pltpu.VMEM((SPAN, SPAN), BF16),
            pltpu.VMEM((PER_GROUP, STATE), F32),
            pltpu.VMEM((2, SPAN, WIDTH), BF16),
            pltpu.VMEM((SPAN, SPAN), F32),
            pltpu.VMEM((SPAN, WIDTH), F32),
            dma((max(cache_n - 1, 1),)),
            dma((max(cache_n - 1, 1),)),
            dma((requests,)),
            dma((requests, tok_n)),
            dma((units,)),
            dma((units,)),
            dma((requests, tok_n)),
            dma((requests,)),
        ],
        compiler_params=pltpu.CompilerParams(
            collective_id=0, has_side_effects=True, vmem_limit_bytes=60 * 1024 * 1024
        ),
        cost_estimate=pl.CostEstimate(
            flops=units * 14 * SPAN * SPAN * WIDTH,
            bytes_accessed=units * SPAN * WIDTH * 8,
            transcendentals=units * PER_GROUP * SPAN * SPAN,
        ),
    )(
        parent,
        state_dev,
        state_slot,
        spans,
        step_t,
        rate_t,
        skip_w,
        norm_w[None, :],
        x_in,
        z_in,
        b_in.reshape(requests, segment, groups * STATE),
        c_in.reshape(requests, segment, groups * STATE),
        cache_states.reshape(slots, cache_n, owned, STATE),
    )
    return (y_out, final_states.reshape(requests, heads // tok_n, HEAD_DIM, STATE))


def solution(mesh):
    placed = (
        P(("groups", "rep"), "tok", "cache"),
        P(("groups", "rep"), "tok", "cache"),
        P(("groups", "rep"), "tok", "cache", None),
        P(("groups", "rep"), "tok", "cache", None),
        P(("groups", "rep"), "tok", "cache"),
        P("cache"),
        P("cache"),
        P("cache"),
        P("cache"),
        P(("groups", "cache"), None, "tok", None, None),
        P("groups"),
        P("groups"),
        P("groups"),
        P("groups"),
    )
    return jax.shard_map(
        shards,
        mesh=mesh,
        in_specs=placed,
        out_specs=(
            P(("groups", "rep"), "tok", "cache"),
            P(("groups", "rep"), ("cache", "tok"), None, None),
        ),
        check_vma=False,
    )
```

time: 403 us -> 195 us (0.48); the launches traced: 398 us -> 195 us
  waiting for transfers between devices: 220 us -> 0 us
  Pallas kernels: 0 us -> 180 us
  local copies, waits for them, and re-layouts: 79.3 us -> 12.3 us
  other arithmetic: 38.7 us -> 2.3 us
  matrix products: 26 us -> 0 us
  starting transfers between devices: 17.9 us -> 0 us
  between operations: 15.8 us -> 0.65 us
    pallas_call x0 -> x1, Pallas kernels: none -> 180 us  [shards(): pl.pallas_call(functools.partial(scan_kernel, tok_n, cache_n, requests, g...]
    all_gather x2 -> x0, waiting for transfers between devices: 96.1 us -> none  [the longest x1 91.3 us: shards(): lax.all_gather(c_in, 'tok', axis=1, tiled=True)]
    all_to_all x3 -> x0, waiting for transfers between devices: 87.5 us -> none  [the longest x1 84.7 us: shards(): lax.all_to_all(ssd, 'tok', split_axis=1, concat_axis=2, tiled=True)]
    unnamed x4 -> x0, waiting for transfers between devices: 36.2 us -> none
    dot_general x4 -> x0, matrix products: 26 us -> none  [the longest x1 9.13 us: span_scan(): jnp.einsum('mkhij,mkjhp->mkihp', blend_factors, x_blocks, preferred_eleme...]
    reshape x2, local copies, waits for them, and re-layouts: 25.8 us -> 4.06 us  [the longest x1 2.03 us: shards(): c_in.reshape(requests, segment, groups * STATE)]
    unnamed x47 -> x4, local copies, waits for them, and re-layouts: 26.5 us -> 6.17 us
    all_to_all x3 -> x0, starting transfers between devices: 17.8 us -> none  [the longest x1 7.66 us: shards(): lax.all_to_all(ssd, 'tok', split_axis=1, concat_axis=2, tiled=True)]
  transfers between devices with their start and end apart: 6 -> 0, of which waited for: 5 -> 0; matrix products, arithmetic and copies ran while one was open for 8% -> 0% of each run, Pallas kernels for 0% -> 0%
where the time goes in v1:
time: 195 us
  Pallas kernels  180 us (92%)
  local copies, waits for them, and re-layouts  12.3 us (6%)
  other arithmetic  2.3 us (1%)
    pallas_call x1, Pallas kernels, shards(): pl.pallas_call(functools.partial(scan_kernel, tok_n, cache_n, requests, g...  180 us
    unnamed x4, local copies, waits for them, and re-layouts  6.17 us

profile of v1, /device:TPU:24, one launch (start us, length us, event | category | flops | bytes accessed | tf_op | source)
XLA Modules:
  0.0 194.9 jit_solution(3204047049555499969)
XLA Ops:
  0.6 0.7 exponential_negate_fusion
  1.3 0.7 broadcast_in_dim.6.rate_t
  2.0 0.7 broadcast_in_dim.14
  2.7 0.7 broadcast_in_dim_reshape.3.skip_w
  3.4 1.6 fusion.step_t
  5.0 2.0 %reshape.19.b_in = bf16[4,128,512]{2,1,0:T(8,128)(2,1)} reshape(bf16[4,128,4,128]{3,2,1,0:T(4,128)(2,1)} %param.16) | data formatting | bytes 1048576 | tf_op jit(solution)/shard_map/reshape | solution.py:407
  7.1 2.0 %reshape.20.c_in = bf16[4,128,512]{2,1,0:T(8,128)(2,1)} reshape(bf16[4,128,4,128]{3,2,1,0:T(4,128)(2,1)} %param.17) | data formatting | bytes 1048576 | tf_op jit(solution)/shard_map/reshape | solution.py:408
  9.1 179.7 %shard_map.149 = (bf16[4,128,4096]{2,1,0:T(8,128)(2,1)}, f32[4,1024,128]{2,1,0:T(8,128)}) custom-call(s32[8]{0:T(128)} %parent.1, s32[4]{0:T(128)} %state_dev.1, s32[4]{0:T(128)} %state_slot.1, s32[8]{0:T(128)} %spans.1, f32[4,64,128]{2,1,0:T(8,128)} %fusion.step_t, f32[64,128]{1,0:T(8,128)} %broadcast_in_dim.6.rate_t, ...), custom_call_target="tpu_custom_call" | custom-call | flops 3758096384 | bytes 16777216 | tf_op jit(solution)/shard_map/pallas_call | solution.py:357
  188.8 0.0 copy-start
  188.8 4.8 %copy.18 = bf16[4,128,4096]{2,1,0:T(8,128)(2,1)} copy(bf16[4,128,4096]{2,1,0:T(8,128)(2,1)} %get-tuple-element.8) | data formatting | bytes 8388608
  193.6 0.0 copy-done
  193.6 1.3 copy.19
Async XLA Ops:
  188.8 4.9 %copy-start = (f32[4,1024,128]{2,1,0:T(8,128)S(1)}, f32[4,1024,128]{2,1,0:T(8,128)}, u32[]{:S(2)}) copy-start(f32[4,1024,128]{2,1,0:T(8,128)} %get-tuple-element.5) | copy-start | bytes 6291460

commit v2 on v1

--- a/solution.py
+++ b/solution.py
@@ -272,6 +272,7 @@
 
     for d in range(1, cache_n):
         kept_copy(d).wait_recv()
+    sent_at = [(groups - 1) * r - 2 for r in range(requests)]
     my_group = t // pieces
     my_piece = lax.rem(t, pieces)
     for r in range(requests):
@@ -286,10 +287,18 @@
         @pl.when(t > 0)
         def _():
             initial[r] = state
-            init_copy(r, unit_of(r, my_group), my_piece, t).start()
+            if sent_at[r] < 0:
+                init_copy(r, unit_of(r, my_group), my_piece, t).start()
 
     @pl.loop(0, units)
     def _(u):
+        for r in range(requests):
+            if sent_at[r] >= 0:
+
+                @pl.when((t > 0) & (u == sent_at[r]))
+                def _():
+                    init_copy(r, unit_of(r, my_group), my_piece, t).start()
+
         prepare(u)
         advance(u)
 

time: 195 us -> 184 us (0.944)
  Pallas kernels: 180 us -> 168 us
    pallas_call x1, Pallas kernels: 180 us -> 168 us  [shards(): pl.pallas_call(functools.partial(scan_kernel, tok_n, cache_n, requests, g...]
where the time goes in v2:
time: 184 us
  Pallas kernels  168 us (91%)
  local copies, waits for them, and re-layouts  12.3 us (7%)
  other arithmetic  2.3 us (1%)
    pallas_call x1, Pallas kernels, shards(): pl.pallas_call(functools.partial(scan_kernel, tok_n, cache_n, requests, g...  168 us
    unnamed x4, local copies, waits for them, and re-layouts  6.17 us

profile of v2, /device:TPU:24, one launch (start us, length us, event | category | flops | bytes accessed | tf_op | source)
XLA Modules:
  0.0 183.7 jit_solution(4862546496728144285)
XLA Ops:
  0.6 0.7 exponential_negate_fusion
  1.3 0.7 broadcast_in_dim.6.rate_t
  2.0 0.7 broadcast_in_dim.14
  2.7 0.7 broadcast_in_dim_reshape.3.skip_w
  3.4 1.6 fusion.step_t
  5.0 2.0 %reshape.19.b_in = bf16[4,128,512]{2,1,0:T(8,128)(2,1)} reshape(bf16[4,128,4,128]{3,2,1,0:T(4,128)(2,1)} %param.16) | data formatting | bytes 1048576 | tf_op jit(solution)/shard_map/reshape | solution.py:416
  7.1 2.0 %reshape.20.c_in = bf16[4,128,512]{2,1,0:T(8,128)(2,1)} reshape(bf16[4,128,4,128]{3,2,1,0:T(4,128)(2,1)} %param.17) | data formatting | bytes 1048576 | tf_op jit(solution)/shard_map/reshape | solution.py:417
  9.1 168.4 %shard_map.149 = (bf16[4,128,4096]{2,1,0:T(8,128)(2,1)}, f32[4,1024,128]{2,1,0:T(8,128)}) custom-call(s32[8]{0:T(128)} %parent.1, s32[4]{0:T(128)} %state_dev.1, s32[4]{0:T(128)} %state_slot.1, s32[8]{0:T(128)} %spans.1, f32[4,64,128]{2,1,0:T(8,128)} %fusion.step_t, f32[64,128]{1,0:T(8,128)} %broadcast_in_dim.6.rate_t, ...), custom_call_target="tpu_custom_call" | custom-call | flops 3758096384 | bytes 16777216 | tf_op jit(solution)/shard_map/pallas_call | solution.py:366
  177.5 0.0 copy-start
  177.5 4.8 %copy.18 = bf16[4,128,4096]{2,1,0:T(8,128)(2,1)} copy(bf16[4,128,4096]{2,1,0:T(8,128)(2,1)} %get-tuple-element.8) | data formatting | bytes 8388608
  182.4 0.0 copy-done
  182.4 1.3 copy.19
Async XLA Ops:
  177.5 4.9 %copy-start = (f32[4,1024,128]{2,1,0:T(8,128)S(1)}, f32[4,1024,128]{2,1,0:T(8,128)}, u32[]{:S(2)}) copy-start(f32[4,1024,128]{2,1,0:T(8,128)} %get-tuple-element.5) | copy-start | bytes 6291460
